TPU v7x, 256 devices: a whole 4x4x8 slice. The times are simulated.
256 devices in a mesh: dp: 8 (over y, core), shard: 32 (over z, x).
Axes of the slice: x: 4, y: 4, z: 8, core: 2. Of those that a mesh axis runs over, the one named last changes fastest.
Arguments:
- grads: bfloat16 [104, 1024, 704], P(None, 'shard'), may hold values from -150 to 150
- momentum: bfloat16 [256, 1024, 704], P(('dp', 'shard')), may hold values from -24 to 24
- owners: int32 [104], replicated, may hold values from 0 to 255, as said below
Outputs:
- updates: bfloat16 [104, 1024, 704], P(None, 'shard')
- momentum_next: bfloat16 [256, 1024, 704], P(('dp', 'shard'))
Inputs may be any that keep to these rules, and one draw needn't show every extreme that they name: `owners`: device d is the one with dp index d // 32 and shard index d % 32. Each device owns at most 1 matrices, and some device owns exactly 1.
All inputs are finite; a program needn't handle non-finite values.
Results may differ from a plain program's by a relative error of at most 0.0058.
Values may be sent and summed in bfloat16 or wider, within the bound.
No kernel may reach another device: no remote copies, remote signals or barrier semaphores. Data moves between devices by JAX's collectives and lax.ppermute only.
A program may use at most 128 MiB of HBM per device.

v0:
```python
import functools
import math

import jax
import jax.numpy as jnp
from jax import lax
from jax.experimental import pallas as pl
from jax.experimental.pallas import tpu as pltpu
from jax.sharding import PartitionSpec as P

DECAY = 0.95
LINEAR, CUBIC, QUINTIC = 3.4445, -4.775, 2.0315
EPS = 1e-07
ITERS = 2
AXES = ("dp", "shard")
NZ, NX, NC, NY = 8, 4, 2, 4
SHARDS = NZ * NX
GROUPS = NY * NC
NT = (((1,), (1,)), ((), ()))
NN = (((1,), (0,)), ((), ()))
ANY = pl.BlockSpec(memory_space=pl.ANY)
HBM = pl.BlockSpec(memory_space=pltpu.HBM)
SMEM = pl.BlockSpec(memory_space=pltpu.SMEM)
VMEM = pl.BlockSpec(memory_space=pltpu.VMEM)


def seat(z, x):
    pick = jnp.where if isinstance(z, jax.Array) else (lambda c, a, b: a if c else b)
    return pick(z < NZ // 2, 2 * z, 2 * NZ - 1 - 2 * z) + NZ * pick(x < NX // 2, 2 * x, 2 * NX - 1 - 2 * x)


SEATED = sorted(range(SHARDS), key=lambda s: seat(s // NX, s % NX))
MEMBERS = [[g * SHARDS + s for s in SEATED] for g in range(GROUPS)]


def hop_y(array, step):
    count, along = GROUPS * SHARDS, NC * SHARDS
    return lax.ppermute(array, AXES, [(d, (d + along * step) % count) for d in range(count)])


def hop_core(array):
    return lax.ppermute(array, AXES, [(d, d ^ SHARDS) for d in range(GROUPS * SHARDS)])


LANES = 128


def put_dense(out, index, block):
    n, columns = block.shape
    whole = columns // LANES
    for tile in range(whole):
        out[index, tile * n : (tile + 1) * n] = block[:, tile * LANES : (tile + 1) * LANES]
    rest = block[:, whole * LANES :]
    out[index, whole * n :] = jnp.concatenate([rest[: n // 2], rest[n // 2 :]], axis=1)


def get_dense(blocks, index, n):
    whole = blocks.shape[1] // n
    tiles = [blocks[index, tile * n : (tile + 1) * n] for tile in range(whole)]
    rest = blocks[index, whole * n :]
    return tiles + [jnp.concatenate([rest[:, : LANES // 2], rest[:, LANES // 2 :]], axis=0)]


def dense_rows(n, columns):
    return n * columns // LANES


def pack_kernel(owners, group, grads, out, rows, dense, places, sems, back):
    count, unroll = owners.shape[0], 8

    def copy(m, k):
        return pltpu.make_async_copy(grads.at[m], rows.at[k], sems.at[k])

    def look(m, found):
        owner = owners[m]
        mine = (owner >> 5) == group[0]

        @pl.when(mine)
        def _():
            copy(m, found).start()
            places[found] = seat((owner >> 2) & (NZ - 1), owner & (NX - 1))

        return found + mine.astype(jnp.int32)

    def look_many(i, found):
        for j in range(unroll):
            found = look(i * unroll + j, found)
        return found

    found = lax.fori_loop(0, count // unroll, look_many, jnp.int32(0))
    for m in range(count // unroll * unroll, count):
        found = look(m, found)

    def send(k):
        return pltpu.make_async_copy(dense.at[k], out.at[places[k]], back.at[k])

    def store(k, carry):
        copy(0, k).wait()
        put_dense(dense, k, rows[k])
        send(k).start()
        return carry

    def finish(k, carry):
        send(k).wait()
        return carry

    lax.fori_loop(0, found, store, 0)
    lax.fori_loop(0, found, finish, 0)


def pack(owners, group, grads):
    _, rows, columns = grads.shape
    return pl.pallas_call(
        pack_kernel,
        out_shape=jax.ShapeDtypeStruct((SHARDS, dense_rows(rows, columns), LANES), grads.dtype),
        in_specs=[SMEM, SMEM, HBM],
        out_specs=HBM,
        scratch_shapes=[
            pltpu.VMEM((SHARDS, rows, columns), grads.dtype),
            pltpu.VMEM((SHARDS, dense_rows(rows, columns), LANES), grads.dtype),
            pltpu.SMEM((SHARDS,), jnp.int32),
            pltpu.SemaphoreType.DMA((SHARDS,)),
            pltpu.SemaphoreType.DMA((SHARDS,)),
        ],
        compiler_params=pltpu.CompilerParams(vmem_limit_bytes=56 * 2**20),
        name="pack_rows",
    )(owners, group, grads)


def dot(a, b, dims):
    return lax.dot_general(a, b, dims, preferred_element_type=jnp.float32)


def step_kernel(scale, owned_ref, rows_ref, mom_ref, out_ref, next_hbm, blend, cur, gram, poly, next_ref, sem):
    rows = mom_ref.shape[1] // SHARDS
    span = NX * rows
    owned = owned_ref[0] > 0
    total = jnp.zeros((8, span), jnp.float32)
    for z in range(NZ):
        cols = slice(z * span, (z + 1) * span)
        tiles = zip(*[get_dense(rows_ref, seat(z, x), rows) for x in range(NX)])
        grad = jnp.concatenate([jnp.concatenate(tile, axis=0) for tile in tiles], axis=1)
        grad = jnp.where(owned, grad.T.astype(jnp.float32), 0.0)
        renewed = DECAY * mom_ref[:, cols].astype(jnp.float32) + grad
        next_ref[:, cols] = renewed.astype(jnp.bfloat16)
        mixed = grad + DECAY * renewed
        blend[:, cols] = mixed
        total = total + jnp.sum((mixed * mixed).reshape(-1, 8, span), axis=0)
    keep = pltpu.make_async_copy(next_ref, next_hbm, sem)
    keep.start()
    inverse = 1.0 / (jnp.sqrt(jnp.sum(total)) + EPS)
    cur[...] = (blend[...] * inverse).astype(jnp.bfloat16)
    columns, total_rows = cur.shape
    cuts = [(low, min(low + 256, columns)) for low in range(0, columns, 256)]
    wide = 2 * span
    for iteration in range(ITERS):
        for low, high in cuts:
            block = dot(cur[:high], cur[low:high], NT).astype(jnp.bfloat16)
            gram[:high, low:high] = block
            if low:
                gram[low:high, :low] = block[:low].T
        for low, high in cuts:
            square = dot(gram[:high], gram[:, low:high], NN)
            block = (CUBIC * gram[:high, low:high].astype(jnp.float32) + QUINTIC * square).astype(jnp.bfloat16)
            poly[:high, low:high] = block
            if low:
                poly[low:high, :low] = block[:low].T
        factor = poly[...]
        if iteration + 1 < ITERS:
            x = cur[...]
            cur[...] = (LINEAR * x.astype(jnp.float32) + dot(factor, x, NN)).astype(jnp.bfloat16)
            continue
        for left in range(0, total_rows, wide):
            x = cur[:, left : left + wide]
            last = (scale * LINEAR) * x.astype(jnp.float32) + scale * dot(factor, x, NN)
            last = last.astype(jnp.bfloat16)
            for z in range(left // span, (left + wide) // span):
                update = last[:, z * span - left : (z + 1) * span - left].T
                for x in range(NX):
                    put_dense(out_ref, seat(z, x), update[x * rows : (x + 1) * rows])
    keep.wait()


def muon_step(owned, rows, momentum_t):
    columns, total_rows = momentum_t.shape
    scale = 0.2 * math.sqrt(max(columns, total_rows))
    square = pltpu.VMEM((columns, columns), jnp.bfloat16)
    return pl.pallas_call(
        functools.partial(step_kernel, scale),
        out_shape=(
            jax.ShapeDtypeStruct(rows.shape, jnp.bfloat16),
            jax.ShapeDtypeStruct(momentum_t.shape, jnp.bfloat16),
        ),
        in_specs=[SMEM, VMEM, VMEM],
        out_specs=(VMEM, HBM),
        scratch_shapes=[
            pltpu.VMEM(momentum_t.shape, jnp.float32),
            pltpu.VMEM(momentum_t.shape, jnp.bfloat16),
            square,
            square,
            pltpu.VMEM(momentum_t.shape, jnp.bfloat16),
            pltpu.SemaphoreType.DMA,
        ],
        compiler_params=pltpu.CompilerParams(vmem_limit_bytes=24 * 2**20),
        name="newton_schulz",
    )(owned, rows, momentum_t)


def select_kernel(seats, order, counts, where, blocks, out):
    group = where[0]

    def body(k, carry):
        out[k] = blocks[seats[order[group * SHARDS + k]]]
        return carry

    lax.fori_loop(0, counts[group], body, 0)


def select(seats, order, counts, where, blocks, slots):
    return pl.pallas_call(
        select_kernel,
        out_shape=jax.ShapeDtypeStruct((slots,) + blocks.shape[1:], blocks.dtype),
        in_specs=[SMEM] * 4 + [VMEM],
        out_specs=VMEM,
        compiler_params=pltpu.CompilerParams(vmem_limit_bytes=16 * 2**20),
        name="select_blocks",
    )(seats, order, counts, where, blocks)


def place_kernel(origins, order, counts, where, *refs):
    pieces, (out, rows, sems) = refs[: len(origins)], refs[-3:]
    height = out.shape[1]
    offsets = [sum(piece.shape[0] for piece in pieces[:i]) for i in range(len(pieces))]

    def unpack(chosen, k, carry):
        for i in chosen:
            for tile, value in enumerate(get_dense(pieces[i], k, height)):
                left = tile * LANES
                rows[offsets[i] + k, :, left : left + value.shape[1]] = value
        return carry

    homes = [((where[0] ^ core) + NC * hop) & (GROUPS - 1) for core, hop, _ in origins]

    def copy(i, k):
        m = order[homes[i] * SHARDS + origins[i][2] + k]
        return pltpu.make_async_copy(rows.at[offsets[i] + k], out.at[m], sems.at[m])

    def start(chosen, k, carry):
        unpack(chosen, k, carry)
        for i in chosen:
            pl.when(origins[i][2] + k < counts[homes[i]])(lambda i=i: copy(i, k).start())
        return carry

    done = 0
    for size in sorted({piece.shape[0] for piece in pieces}):
        chosen = [i for i, piece in enumerate(pieces) if piece.shape[0] >= size]
        lax.fori_loop(done, size, functools.partial(start, chosen), 0)
        done = size

    for i, piece in enumerate(pieces):

        def wait(k, carry, i=i):
            copy(i, k).wait()
            return carry

        lax.fori_loop(0, jnp.minimum(counts[homes[i]] - origins[i][2], piece.shape[0]), wait, 0)


def place(origins, order, counts, where, pieces, shape, base=None):
    bases = [] if base is None else [base]
    slots = sum(piece.shape[0] for piece in pieces)
    return pl.pallas_call(
        functools.partial(place_kernel, origins),
        out_shape=jax.ShapeDtypeStruct(shape, pieces[0].dtype),
        in_specs=[SMEM] * 3 + [VMEM] * len(pieces) + [HBM] * len(bases),
        out_specs=HBM,
        input_output_aliases={3 + len(pieces): 0} if bases else {},
        scratch_shapes=[
            pltpu.VMEM((slots,) + shape[1:], pieces[0].dtype),
            pltpu.SemaphoreType.DMA((shape[0],)),
        ],
        compiler_params=pltpu.CompilerParams(vmem_limit_bytes=16 * 2**20),
        name="place_blocks",
    )(order, counts, where, *pieces, *bases)


def spread(slots, shape, seats, order, counts, where, blocks):
    split = (slots + 1) // 2
    own = select(seats, order, counts, where, blocks, slots)
    low, high = own[:split], own[split:]
    below_low, above_high = hop_y(low, 1), hop_y(high, -1)
    below_high, above_low = hop_y(high, 1), hop_y(low, -1)
    far = [hop_y(below_low, 1), hop_y(above_high, -1)]
    def at(core, origins):
        return [(core, *origin) for origin in origins]

    tables = (order, counts, where)
    early = lax.optimization_barrier([own, below_low, above_high])
    early_origins = [(0, 0), (3, 0), (1, split)]
    late_origins = [(3, split), (1, 0), (2, 0), (2, split)]
    updates = place(at(0, early_origins), *tables, early, shape)
    updates, *late = lax.optimization_barrier([updates, below_high, above_low] + far)
    early_other = [hop_core(piece) for piece in early]
    late_other = [hop_core(piece) for piece in late]
    origins = at(1, early_origins) + at(0, late_origins)
    updates = place(origins, *tables, early_other + late, shape, updates)
    return place(at(1, late_origins), *tables, late_other, shape, updates)


def on_device(grads, momentum, owners):
    count = owners.shape[0]
    group = lax.axis_index("dp")
    me = lax.axis_index(AXES)
    where = group[None].astype(jnp.int32)
    packed = pack(owners, where, grads)
    rows = lax.all_to_all(packed, AXES, 0, 0, tiled=True, axis_index_groups=MEMBERS)

    ids = jnp.arange(count, dtype=jnp.int32)
    homes = owners // SHARDS
    seats = seat((owners >> 2) & (NZ - 1), owners & (NX - 1))
    before = (homes[:, None] == homes[None, :]) & (owners[None, :] < owners[:, None])
    slot = homes * SHARDS + jnp.sum(before.astype(jnp.int32), axis=1)
    order = jnp.sum(
        jnp.where(slot[None, :] == jnp.arange(GROUPS * SHARDS, dtype=jnp.int32)[:, None], ids[None, :], 0), axis=1
    )
    counts = jnp.sum((homes[None, :] == jnp.arange(GROUPS, dtype=jnp.int32)[:, None]).astype(jnp.int32), axis=1)
    owned = jnp.any(owners == me)[None].astype(jnp.int32)

    blocks, following = muon_step(owned, rows, momentum[0].T)
    blocks = lax.all_to_all(blocks, AXES, 0, 0, tiled=True, axis_index_groups=MEMBERS)
    few = 19
    updates = lax.cond(
        jnp.max(counts) <= few,
        functools.partial(spread, few, grads.shape),
        functools.partial(spread, SHARDS, grads.shape),
        seats,
        order,
        counts,
        where,
        blocks,
    )
    return (updates, following.T[None])


def solution(mesh):
    return jax.shard_map(
        on_device,
        mesh=mesh,
        in_specs=(P(None, "shard", None), P(AXES, None, None), P()),
        out_specs=(P(None, "shard", None), P(AXES, None, None)),
        check_vma=False,
    )
```

profile of v0, /device:TPU:33, one launch (start us, length us, event | category | flops | bytes accessed | tf_op | source)
XLA Modules:
  0.0 143.8 jit_solution(6034489781244529109)
XLA Ops:
  0.6 3.9 %pack_rows.1 = bf16[32,176,128]{2,1,0:T(8,128)(2,1)} custom-call(s32[104]{0:T(128)} %owners.1, s32[1]{0:T(128)} %bitcast.group, bf16[104,32,704]{2,1,0:T(8,128)(2,1)} %grads.1), custom_call_target="tpu_custom_call" | custom-call | tf_op jit(solution)/shard_map/pack_rows/pallas_call | solution.py:113
  4.5 0.0 copy-start.2
  4.6 10.8 %all-to-all-start = ((bf16[32,176,128]{2,1,0:T(8,128)(2,1)}), bf16[32,176,128]{2,1,0:T(8,128)(2,1)S(1)}, u32[]{:S(2)}, u32[]{:S(2)}) async-start(bf16[32,176,128]{2,1,0:T(8,128)(2,1)} %pack_rows.1), calls=%async_computation | async-start | bytes 2883584 | tf_op jit(solution)/shard_map/all_to_all | solution.py:316
  15.3 0.6 compare_reduce_fusion
  16.6 35.6 %all-to-all-done.rows_ref = bf16[32,176,128]{2,1,0:T(8,128)(2,1)S(1)} async-done(((bf16[32,176,128]{2,1,0:T(8,128)(2,1)}), bf16[32,176,128]{2,1,0:T(8,128)(2,1)S(1)}, u32[]{:S(2)}, u32[]{:S(2)}) %all-to-all-start) | async-done | bytes 1441824 | tf_op jit(solution)/shard_map/all_to_all | solution.py:316
  52.2 7.3 %newton_schulz.1 = (bf16[32,176,128]{2,1,0:T(8,128)(2,1)S(1)}, bf16[704,1024]{1,0:T(8,128)(2,1)}) custom-call(s32[1]{0:T(128)} %bitcast.1.owned_ref, bf16[32,176,128]{2,1,0:T(8,128)(2,1)S(1)} %all-to-all-done.rows_ref, bf16[704,1024]{1,0:T(8,128)(2,1)S(1)} %bitcast.8), custom_call_target="tpu_custom_call" | custom-call | tf_op jit(solution)/shard_map/newton_schulz/pallas_call | solution.py:188
  59.5 1.1 copy-done.1
  60.6 5.0 %all-to-all-start.1 = ((bf16[32,176,128]{2,1,0:T(8,128)(2,1)}), bf16[32,176,128]{2,1,0:T(8,128)(2,1)S(1)}, u32[]{:S(2)}, u32[]{:S(2)}) async-start(bf16[32,176,128]{2,1,0:T(8,128)(2,1)} %copy-done.1), calls=%async_computation.1 | async-start | bytes 2883584 | tf_op jit(solution)/shard_map/all_to_all | solution.py:330
  65.6 0.1 convert_reduce_fusion.1
  65.7 0.6 reduce_max.9
  67.0 0.2 convert_reduce_fusion
  67.2 0.1 select_reduce_fusion
  67.3 35.2 %all-to-all-done.1 = bf16[32,176,128]{2,1,0:T(8,128)(2,1)S(1)} async-done(((bf16[32,176,128]{2,1,0:T(8,128)(2,1)}), bf16[32,176,128]{2,1,0:T(8,128)(2,1)S(1)}, u32[]{:S(2)}, u32[]{:S(2)}) %all-to-all-start.1) | async-done | bytes 1441824 | tf_op jit(solution)/shard_map/all_to_all | solution.py:330
  102.5 41.1 %conditional.1 = (bf16[104,32,704]{2,1,0:T(8,128)(2,1)}) conditional(s32[]{:T(128)} %convert_element_type.15, (s32[104]{0:T(128)S(1)}, s32[256]{0:T(256)S(1)}, s32[8]{0:T(128)S(1)}, s32[1]{0:T(128)}, bf16[32,176,128]{2,1,0:T(8,128)(2,1)S(1)}) %tuple.18, (s32[104]{0:T(128)S(1)}, s32[256]{0:T(256)S(1)}, s32[8]{0:T(128)S(1)}, s32[1]{0:T(128)}, ...), branch_computations={%region_5.6_spmd, %region_6.7_spmd} | conditional | bytes 43254288 | solution.py:332
  102.5 0.7 select_blocks.3.refs_0_
  103.3 1.5 %collective-permute-start = (bf16[10,176,128]{2,1,0:T(8,128)(2,1)S(1)}, bf16[10,176,128]{2,1,0:T(8,128)(2,1)S(1)}, u32[]{:S(2)}, u32[]{:S(2)}) collective-permute-start(bf16[10,176,128]{2,1,0:T(8,128)(2,1)S(1)} %slice.14), channel_id=1, source_target_pairs={{0,64},{1,65},{2,66},{3,67},{4,68},{5,69},{6,70},{7,71},{8,72},{9,... | collective-permute-start | bytes 1351688 | tf_op jit(solution)/shard_map/cond/branch_1_fun/ppermute | solution.py:38
  104.8 1.3 collective-permute-start.1
  106.1 1.1 collective-permute-start.3
  107.2 0.4 collective-permute-start.2
  107.6 6.7 %collective-permute-done.refs_1_ = bf16[10,176,128]{2,1,0:T(8,128)(2,1)S(1)} collective-permute-done((bf16[10,176,128]{2,1,0:T(8,128)(2,1)S(1)}, bf16[10,176,128]{2,1,0:T(8,128)(2,1)S(1)}, u32[]{:S(2)}, u32[]{:S(2)}) %collective-permute-start) | collective-permute-done | bytes 450592 | tf_op jit(solution)/shard_map/cond/branch_1_fun/ppermute | solution.py:38
  114.3 0.3 collective-permute-start.4
  114.6 2.3 %collective-permute-start.5 = (bf16[9,176,128]{2,1,0:T(8,128)(2,1)S(1)}, bf16[9,176,128]{2,1,0:T(8,128)(2,1)S(1)}, u32[]{:S(2)}, u32[]{:S(2)}) collective-permute-start(bf16[9,176,128]{2,1,0:T(8,128)(2,1)S(1)} %collective-permute-done.1.refs_2_), channel_id=1, source_target_pairs={{0,192},{1,193},{2,194},{3,195},{4,196},{5,197},{6,198},{7,199},{8... | collective-permute-start | bytes 1216520 | tf_op jit(solution)/shard_map/cond/branch_1_fun/ppermute | solution.py:38
  117.0 6.2 %collective-permute-start.10 = (bf16[19,176,128]{2,1,0:T(8,128)(2,1)S(1)}, bf16[19,176,128]{2,1,0:T(8,128)(2,1)S(1)}, u32[]{:S(2)}, u32[]{:S(2)}) collective-permute-start(bf16[19,176,128]{2,1,0:T(8,128)(2,1)S(1)} %select_blocks.3.refs_0_), channel_id=1, source_target_pairs={{0,32},{1,33},{2,34},{3,35},{4,36},{5,37},{6,38},{7,39},{8,40},{9,... | collective-permute-start | bytes 2568200 | tf_op jit(solution)/shard_map/cond/branch_1_fun/ppermute | solution.py:42
  123.2 5.4 %collective-permute-start.11 = (bf16[10,176,128]{2,1,0:T(8,128)(2,1)S(1)}, bf16[10,176,128]{2,1,0:T(8,128)(2,1)S(1)}, u32[]{:S(2)}, u32[]{:S(2)}) collective-permute-start(bf16[10,176,128]{2,1,0:T(8,128)(2,1)S(1)} %collective-permute-done.refs_1_), channel_id=1, source_target_pairs={{0,32},{1,33},{2,34},{3,35},{4,36},{5,37},{6,38},{7,39},{8,40},{9,... | collective-permute-start | bytes 1351688 | tf_op jit(solution)/shard_map/cond/branch_1_fun/ppermute | solution.py:42
  128.7 0.5 collective-permute-start.12
  129.2 3.3 %place_blocks.9.refs_7_ = bf16[104,32,704]{2,1,0:T(8,128)(2,1)} custom-call(s32[256]{0:T(256)S(1)} %get-tuple-element.36.order, s32[8]{0:T(128)S(1)} %get-tuple-element.37.counts, s32[1]{0:T(128)} %get-tuple-element.38.where, bf16[19,176,128]{2,1,0:T(8,128)(2,1)S(1)} %select_blocks.3.refs_0_, bf16[10,176,128]{2,1,0:T(8,128)(2,1)S(1)} %collective-permute-done.refs_1_, ...), custom_call_target="tpu_custom_call" | custom-call | tf_op jit(solution)/shard_map/cond/branch_1_fun/place_blocks/pallas_call | solution.py:272
  132.5 0.1 collective-permute-done.4.refs_5_
  132.6 3.0 %collective-permute-start.7 = (bf16[10,176,128]{2,1,0:T(8,128)(2,1)S(1)}, bf16[10,176,128]{2,1,0:T(8,128)(2,1)S(1)}, u32[]{:S(2)}, u32[]{:S(2)}) collective-permute-start(bf16[10,176,128]{2,1,0:T(8,128)(2,1)S(1)} %collective-permute-done.3.refs_4_), channel_id=1, source_target_pairs={{0,32},{1,33},{2,34},{3,35},{4,36},{5,37},{6,38},{7,39},{8,40},{9,... | collective-permute-start | bytes 1351688 | tf_op jit(solution)/shard_map/cond/branch_1_fun/ppermute | solution.py:42
  135.7 0.5 collective-permute-start.6
  136.2 0.1 collective-permute-start.9
  136.3 4.1 %place_blocks.10.refs_4_ = bf16[104,32,704]{2,1,0:T(8,128)(2,1)} custom-call(s32[256]{0:T(256)S(1)} %get-tuple-element.36.order, s32[8]{0:T(128)S(1)} %get-tuple-element.37.counts, s32[1]{0:T(128)} %get-tuple-element.38.where, bf16[19,176,128]{2,1,0:T(8,128)(2,1)S(1)} %collective-permute-done.10.refs_0_, ...), custom_call_target="tpu_custom_call", output_to_operand_aliasing={{}: (10, {})} | custom-call | tf_op jit(solution)/shard_map/cond/branch_1_fun/place_blocks/pallas_call | solution.py:272
  140.5 3.1 %place_blocks.11 = bf16[104,32,704]{2,1,0:T(8,128)(2,1)} custom-call(s32[256]{0:T(256)S(1)} %get-tuple-element.36.order, s32[8]{0:T(128)S(1)} %get-tuple-element.37.counts, s32[1]{0:T(128)} %get-tuple-element.38.where, bf16[9,176,128]{2,1,0:T(8,128)(2,1)S(1)} %collective-permute-done.6.refs_0_, ...), custom_call_target="tpu_custom_call", output_to_operand_aliasing={{}: (7, {})} | custom-call | tf_op jit(solution)/shard_map/cond/branch_1_fun/place_blocks/pallas_call | solution.py:272
  (20 shorter events, 0.1 us)
Async XLA Ops:
  4.5 10.8 %copy-start.2 = (s32[104]{0:T(128)S(1)}, s32[104]{0:T(128)}, u32[]{:S(2)}) copy-start(s32[104]{0:T(128)} %owners.1) | copy-start | bytes 1252
  4.5 47.7 %copy-start = (bf16[1,1024,704]{1,2,0:T(8,128)(2,1)S(1)}, bf16[1,1024,704]{1,2,0:T(8,128)(2,1)}, u32[]{:S(2)}) copy-start(bf16[1,1024,704]{1,2,0:T(8,128)(2,1)} %param.6) | copy-start | bytes 4325380
  4.6 47.7 %all-to-all-start = ((bf16[32,176,128]{2,1,0:T(8,128)(2,1)}), bf16[32,176,128]{2,1,0:T(8,128)(2,1)S(1)}, u32[]{:S(2)}, u32[]{:S(2)}) async-start(bf16[32,176,128]{2,1,0:T(8,128)(2,1)} %pack_rows.1), calls=%async_computation | async-start | bytes 2883584 | tf_op jit(solution)/shard_map/all_to_all | solution.py:316
  59.5 1.1 copy-start.1
  60.6 41.9 %all-to-all-start.1 = ((bf16[32,176,128]{2,1,0:T(8,128)(2,1)}), bf16[32,176,128]{2,1,0:T(8,128)(2,1)S(1)}, u32[]{:S(2)}, u32[]{:S(2)}) async-start(bf16[32,176,128]{2,1,0:T(8,128)(2,1)} %copy-done.1), calls=%async_computation.1 | async-start | bytes 2883584 | tf_op jit(solution)/shard_map/all_to_all | solution.py:330
  103.3 11.0 %collective-permute-start = (bf16[10,176,128]{2,1,0:T(8,128)(2,1)S(1)}, bf16[10,176,128]{2,1,0:T(8,128)(2,1)S(1)}, u32[]{:S(2)}, u32[]{:S(2)}) collective-permute-start(bf16[10,176,128]{2,1,0:T(8,128)(2,1)S(1)} %slice.14), channel_id=1, source_target_pairs={{0,64},{1,65},{2,66},{3,67},{4,68},{5,69},{6,70},{7,71},{8,72},{9,... | collective-permute-start | bytes 1351688 | tf_op jit(solution)/shard_map/cond/branch_1_fun/ppermute | solution.py:38
  104.8 9.8 %collective-permute-start.1 = (bf16[9,176,128]{2,1,0:T(8,128)(2,1)S(1)}, bf16[9,176,128]{2,1,0:T(8,128)(2,1)S(1)}, u32[]{:S(2)}, u32[]{:S(2)}) collective-permute-start(bf16[9,176,128]{2,1,0:T(8,128)(2,1)S(1)} %slice.15), channel_id=1, source_target_pairs={{0,192},{1,193},{2,194},{3,195},{4,196},{5,197},{6,198},{7,199},{8... | collective-permute-start | bytes 1216520 | tf_op jit(solution)/shard_map/cond/branch_1_fun/ppermute | solution.py:38
  106.1 22.5 %collective-permute-start.3 = (bf16[10,176,128]{2,1,0:T(8,128)(2,1)S(1)}, bf16[10,176,128]{2,1,0:T(8,128)(2,1)S(1)}, u32[]{:S(2)}, u32[]{:S(2)}) collective-permute-start(bf16[10,176,128]{2,1,0:T(8,128)(2,1)S(1)} %slice.14), channel_id=1, source_target_pairs={{0,192},{1,193},{2,194},{3,195},{4,196},{5,197},{6,198},{7,199},{8... | collective-permute-start | bytes 1351688 | tf_op jit(solution)/shard_map/cond/branch_1_fun/ppermute | solution.py:38
  107.2 16.0 %collective-permute-start.2 = (bf16[9,176,128]{2,1,0:T(8,128)(2,1)S(1)}, bf16[9,176,128]{2,1,0:T(8,128)(2,1)S(1)}, u32[]{:S(2)}, u32[]{:S(2)}) collective-permute-start(bf16[9,176,128]{2,1,0:T(8,128)(2,1)S(1)} %slice.15), channel_id=1, source_target_pairs={{0,64},{1,65},{2,66},{3,67},{4,68},{5,69},{6,70},{7,71},{8,72},{9,... | collective-permute-start | bytes 1216520 | tf_op jit(solution)/shard_map/cond/branch_1_fun/ppermute | solution.py:38
  114.3 18.3 %collective-permute-start.4 = (bf16[10,176,128]{2,1,0:T(8,128)(2,1)S(1)}, bf16[10,176,128]{2,1,0:T(8,128)(2,1)S(1)}, u32[]{:S(2)}, u32[]{:S(2)}) collective-permute-start(bf16[10,176,128]{2,1,0:T(8,128)(2,1)S(1)} %collective-permute-done.refs_1_), channel_id=1, source_target_pairs={{0,64},{1,65},{2,66},{3,67},{4,68},{5,69},{6,70},{7,71},{8,72},{9,... | collective-permute-start | bytes 1351688 | tf_op jit(solution)/shard_map/cond/branch_1_fun/ppermute | solution.py:38
  114.6 17.9 %collective-permute-start.5 = (bf16[9,176,128]{2,1,0:T(8,128)(2,1)S(1)}, bf16[9,176,128]{2,1,0:T(8,128)(2,1)S(1)}, u32[]{:S(2)}, u32[]{:S(2)}) collective-permute-start(bf16[9,176,128]{2,1,0:T(8,128)(2,1)S(1)} %collective-permute-done.1.refs_2_), channel_id=1, source_target_pairs={{0,192},{1,193},{2,194},{3,195},{4,196},{5,197},{6,198},{7,199},{8... | collective-permute-start | bytes 1216520 | tf_op jit(solution)/shard_map/cond/branch_1_fun/ppermute | solution.py:38
  117.0 19.3 %collective-permute-start.10 = (bf16[19,176,128]{2,1,0:T(8,128)(2,1)S(1)}, bf16[19,176,128]{2,1,0:T(8,128)(2,1)S(1)}, u32[]{:S(2)}, u32[]{:S(2)}) collective-permute-start(bf16[19,176,128]{2,1,0:T(8,128)(2,1)S(1)} %select_blocks.3.refs_0_), channel_id=1, source_target_pairs={{0,32},{1,33},{2,34},{3,35},{4,36},{5,37},{6,38},{7,39},{8,40},{9,... | collective-permute-start | bytes 2568200 | tf_op jit(solution)/shard_map/cond/branch_1_fun/ppermute | solution.py:42
  123.2 13.0 %collective-permute-start.11 = (bf16[10,176,128]{2,1,0:T(8,128)(2,1)S(1)}, bf16[10,176,128]{2,1,0:T(8,128)(2,1)S(1)}, u32[]{:S(2)}, u32[]{:S(2)}) collective-permute-start(bf16[10,176,128]{2,1,0:T(8,128)(2,1)S(1)} %collective-permute-done.refs_1_), channel_id=1, source_target_pairs={{0,32},{1,33},{2,34},{3,35},{4,36},{5,37},{6,38},{7,39},{8,40},{9,... | collective-permute-start | bytes 1351688 | tf_op jit(solution)/shard_map/cond/branch_1_fun/ppermute | solution.py:42
  128.7 7.0 %collective-permute-start.12 = (bf16[9,176,128]{2,1,0:T(8,128)(2,1)S(1)}, bf16[9,176,128]{2,1,0:T(8,128)(2,1)S(1)}, u32[]{:S(2)}, u32[]{:S(2)}) collective-permute-start(bf16[9,176,128]{2,1,0:T(8,128)(2,1)S(1)} %collective-permute-done.1.refs_2_), channel_id=1, source_target_pairs={{0,32},{1,33},{2,34},{3,35},{4,36},{5,37},{6,38},{7,39},{8,40},{9,... | collective-permute-start | bytes 1216520 | tf_op jit(solution)/shard_map/cond/branch_1_fun/ppermute | solution.py:42
  132.6 7.8 %collective-permute-start.7 = (bf16[10,176,128]{2,1,0:T(8,128)(2,1)S(1)}, bf16[10,176,128]{2,1,0:T(8,128)(2,1)S(1)}, u32[]{:S(2)}, u32[]{:S(2)}) collective-permute-start(bf16[10,176,128]{2,1,0:T(8,128)(2,1)S(1)} %collective-permute-done.3.refs_4_), channel_id=1, source_target_pairs={{0,32},{1,33},{2,34},{3,35},{4,36},{5,37},{6,38},{7,39},{8,40},{9,... | collective-permute-start | bytes 1351688 | tf_op jit(solution)/shard_map/cond/branch_1_fun/ppermute | solution.py:42
  135.7 4.8 %collective-permute-start.8 = (bf16[10,176,128]{2,1,0:T(8,128)(2,1)S(1)}, bf16[10,176,128]{2,1,0:T(8,128)(2,1)S(1)}, u32[]{:S(2)}, u32[]{:S(2)}) collective-permute-start(bf16[10,176,128]{2,1,0:T(8,128)(2,1)S(1)} %collective-permute-done.4.refs_5_), channel_id=1, source_target_pairs={{0,32},{1,33},{2,34},{3,35},{4,36},{5,37},{6,38},{7,39},{8,40},{9,... | collective-permute-start | bytes 1351688 | tf_op jit(solution)/shard_map/cond/branch_1_fun/ppermute | solution.py:42
  135.7 4.7 %collective-permute-start.6 = (bf16[9,176,128]{2,1,0:T(8,128)(2,1)S(1)}, bf16[9,176,128]{2,1,0:T(8,128)(2,1)S(1)}, u32[]{:S(2)}, u32[]{:S(2)}) collective-permute-start(bf16[9,176,128]{2,1,0:T(8,128)(2,1)S(1)} %collective-permute-done.2.refs_3_), channel_id=1, source_target_pairs={{0,32},{1,33},{2,34},{3,35},{4,36},{5,37},{6,38},{7,39},{8,40},{9,... | collective-permute-start | bytes 1216520 | tf_op jit(solution)/shard_map/cond/branch_1_fun/ppermute | solution.py:42
  136.2 4.2 %collective-permute-start.9 = (bf16[9,176,128]{2,1,0:T(8,128)(2,1)S(1)}, bf16[9,176,128]{2,1,0:T(8,128)(2,1)S(1)}, u32[]{:S(2)}, u32[]{:S(2)}) collective-permute-start(bf16[9,176,128]{2,1,0:T(8,128)(2,1)S(1)} %collective-permute-done.5.refs_6_), channel_id=1, source_target_pairs={{0,32},{1,33},{2,34},{3,35},{4,36},{5,37},{6,38},{7,39},{8,40},{9,... | collective-permute-start | bytes 1216520 | tf_op jit(solution)/shard_map/cond/branch_1_fun/ppermute | solution.py:42
where the time goes:
time: 144 us
  waiting for transfers between devices  77.6 us (54%)
  starting transfers between devices  38.6 us (27%)
  Pallas kernels  22.5 us (16%)
  between operations  2.19 us (2%)
  other arithmetic  1.69 us (1%)
    all_to_all x1, waiting for transfers between devices, on_device(): lax.all_to_all(packed, AXES, 0, 0, tiled=True, axis_index_groups=MEMBERS)  35.6 us
    all_to_all x1, waiting for transfers between devices, on_device(): lax.all_to_all(blocks, AXES, 0, 0, tiled=True, axis_index_groups=MEMBERS)  35.2 us
    ppermute x7, starting transfers between devices, hop_core(): lax.ppermute(array, AXES, [(d, d ^ SHARDS) for d in range(GROUPS * SHARDS)])  15.8 us
    all_to_all x1, starting transfers between devices, on_device(): lax.all_to_all(packed, AXES, 0, 0, tiled=True, axis_index_groups=MEMBERS)  10.8 us
    pallas_call x3, Pallas kernels, place(): pl.pallas_call(functools.partial(place_kernel, origins), out_shape=jax.Sh...  10.6 us
    pallas_call x1, Pallas kernels, muon_step(): pl.pallas_call(functools.partial(step_kernel, scale), out_shape=(jax.Shap...  7.28 us
    ppermute x6, starting transfers between devices, hop_y(): lax.ppermute(array, AXES, [(d, (d + along * step) % count) for d in range...  6.97 us
    ppermute x6, waiting for transfers between devices, hop_y(): lax.ppermute(array, AXES, [(d, (d + along * step) % count) for d in range...  6.83 us
  transfers between devices with their start and end apart: 15, of which 4 were waited for; matrix products, arithmetic and copies ran while one was open for 1% of the time, Pallas kernels for 5%

commit v1 on v0

--- a/solution.py
+++ b/solution.py
@@ -26,7 +26,7 @@
 
 def seat(z, x):
     pick = jnp.where if isinstance(z, jax.Array) else (lambda c, a, b: a if c else b)
-    return pick(z < NZ // 2, 2 * z, 2 * NZ - 1 - 2 * z) + NZ * pick(x < NX // 2, 2 * x, 2 * NX - 1 - 2 * x)
+    return NX * pick(z < NZ // 2, 2 * z, 2 * NZ - 1 - 2 * z) + pick(x < NX // 2, 2 * x, 2 * NX - 1 - 2 * x)
 
 
 SEATED = sorted(range(SHARDS), key=lambda s: seat(s // NX, s % NX))
@@ -131,7 +131,7 @@
     return lax.dot_general(a, b, dims, preferred_element_type=jnp.float32)
 
 
-def step_kernel(scale, owned_ref, rows_ref, mom_ref, out_ref, next_hbm, blend, cur, gram, poly, next_ref, sem):
+def step_kernel(scale, owned_ref, rows_ref, mom_ref, out_hbm, next_hbm, blend, cur, gram, poly, next_ref, out_ref, sem, sems):
     rows = mom_ref.shape[1] // SHARDS
     span = NX * rows
     owned = owned_ref[0] > 0
@@ -148,6 +148,7 @@
         total = total + jnp.sum((mixed * mixed).reshape(-1, 8, span), axis=0)
     keep = pltpu.make_async_copy(next_ref, next_hbm, sem)
     keep.start()
+    sent = []
     inverse = 1.0 / (jnp.sqrt(jnp.sum(total)) + EPS)
     cur[...] = (blend[...] * inverse).astype(jnp.bfloat16)
     columns, total_rows = cur.shape
@@ -178,7 +179,11 @@
                 update = last[:, z * span - left : (z + 1) * span - left].T
                 for x in range(NX):
                     put_dense(out_ref, seat(z, x), update[x * rows : (x + 1) * rows])
-    keep.wait()
+                seats = pl.ds(seat(z, 0), NX)
+                sent.append(pltpu.make_async_copy(out_ref.at[seats], out_hbm.at[seats], sems.at[z]))
+                sent[-1].start()
+    for copy in sent + [keep]:
+        copy.wait()
 
 
 def muon_step(owned, rows, momentum_t):
@@ -192,14 +197,16 @@
             jax.ShapeDtypeStruct(momentum_t.shape, jnp.bfloat16),
         ),
         in_specs=[SMEM, VMEM, VMEM],
-        out_specs=(VMEM, HBM),
+        out_specs=(HBM, HBM),
         scratch_shapes=[
             pltpu.VMEM(momentum_t.shape, jnp.float32),
             pltpu.VMEM(momentum_t.shape, jnp.bfloat16),
             square,
             square,
             pltpu.VMEM(momentum_t.shape, jnp.bfloat16),
+            pltpu.VMEM(rows.shape, jnp.bfloat16),
             pltpu.SemaphoreType.DMA,
+            pltpu.SemaphoreType.DMA((NZ,)),
         ],
         compiler_params=pltpu.CompilerParams(vmem_limit_bytes=24 * 2**20),
         name="newton_schulz",

time: 144 us -> 150 us (1.042)
  the two profiles are of different devices: /device:TPU:33 before, /device:TPU:1 now
where the time goes in v1:
time: 150 us
  waiting for transfers between devices  74.4 us (50%)
  starting transfers between devices  43.4 us (29%)
  Pallas kernels  26.8 us (18%)
  between operations  2.19 us (1%)
  other arithmetic  1.69 us (1%)
    all_to_all x1, waiting for transfers between devices, on_device(): lax.all_to_all(packed, AXES, 0, 0, tiled=True, axis_index_groups=MEMBERS)  34.2 us
    all_to_all x1, waiting for transfers between devices, on_device(): lax.all_to_all(blocks, AXES, 0, 0, tiled=True, axis_index_groups=MEMBERS)  33.4 us
    ppermute x7, starting transfers between devices, hop_core(): lax.ppermute(array, AXES, [(d, d ^ SHARDS) for d in range(GROUPS * SHARDS)])  16.1 us
    all_to_all x1, starting transfers between devices, on_device(): lax.all_to_all(packed, AXES, 0, 0, tiled=True, axis_index_groups=MEMBERS)  12 us
    pallas_call x1, Pallas kernels, muon_step(): pl.pallas_call(functools.partial(step_kernel, scale), out_shape=(jax.Shap...  11.8 us
    pallas_call x3, Pallas kernels, place(): pl.pallas_call(functools.partial(place_kernel, origins), out_shape=jax.Sh...  10.5 us
    ppermute x6, starting transfers between devices, hop_y(): lax.ppermute(array, AXES, [(d, (d + along * step) % count) for d in range...  9.48 us
    ppermute x6, waiting for transfers between devices, hop_y(): lax.ppermute(array, AXES, [(d, (d + along * step) % count) for d in range...  6.74 us
  transfers between devices with their start and end apart: 15, of which 4 were waited for; matrix products, arithmetic and copies ran while one was open for 1% of the time, Pallas kernels for 5%

profile of v1, /device:TPU:1, one launch (start us, length us, event | category | flops | bytes accessed | tf_op | source)
XLA Modules:
  0.0 149.7 jit_solution(6401784875270634817)
XLA Ops:
  0.6 3.7 %pack_rows.1 = bf16[32,176,128]{2,1,0:T(8,128)(2,1)} custom-call(s32[104]{0:T(128)} %owners.1, s32[1]{0:T(128)} %bitcast.group, bf16[104,32,704]{2,1,0:T(8,128)(2,1)} %grads.1), custom_call_target="tpu_custom_call" | custom-call | tf_op jit(solution)/shard_map/pack_rows/pallas_call | solution.py:113
  4.4 0.0 copy-start.2
  4.4 0.0 copy-start
  4.4 12.0 %all-to-all-start = ((bf16[32,176,128]{2,1,0:T(8,128)(2,1)}), bf16[32,176,128]{2,1,0:T(8,128)(2,1)S(1)}, u32[]{:S(2)}, u32[]{:S(2)}) async-start(bf16[32,176,128]{2,1,0:T(8,128)(2,1)} %pack_rows.1), calls=%async_computation | async-start | bytes 2883584 | tf_op jit(solution)/shard_map/all_to_all | solution.py:323
  16.4 0.6 compare_reduce_fusion
  17.7 34.2 %all-to-all-done.rows_ref = bf16[32,176,128]{2,1,0:T(8,128)(2,1)S(1)} async-done(((bf16[32,176,128]{2,1,0:T(8,128)(2,1)}), bf16[32,176,128]{2,1,0:T(8,128)(2,1)S(1)}, u32[]{:S(2)}, u32[]{:S(2)}) %all-to-all-start) | async-done | bytes 1441824 | tf_op jit(solution)/shard_map/all_to_all | solution.py:323
  51.9 11.8 %newton_schulz.1 = (bf16[32,176,128]{2,1,0:T(8,128)(2,1)S(1)}, bf16[704,1024]{1,0:T(8,128)(2,1)}) custom-call(s32[1]{0:T(128)} %bitcast.1.owned_ref, bf16[32,176,128]{2,1,0:T(8,128)(2,1)S(1)} %all-to-all-done.rows_ref, bf16[704,1024]{1,0:T(8,128)(2,1)S(1)} %bitcast.8), custom_call_target="tpu_custom_call" | custom-call | tf_op jit(solution)/shard_map/newton_schulz/pallas_call | solution.py:193
  63.8 1.1 copy-done.1
  64.8 5.8 %all-to-all-start.1 = ((bf16[32,176,128]{2,1,0:T(8,128)(2,1)}), bf16[32,176,128]{2,1,0:T(8,128)(2,1)S(1)}, u32[]{:S(2)}, u32[]{:S(2)}) async-start(bf16[32,176,128]{2,1,0:T(8,128)(2,1)} %copy-done.1), calls=%async_computation.1 | async-start | bytes 2883584 | tf_op jit(solution)/shard_map/all_to_all | solution.py:337
  70.7 0.1 convert_reduce_fusion.1
  70.8 0.6 reduce_max.9
  72.1 0.2 convert_reduce_fusion
  72.3 0.1 select_reduce_fusion
  72.4 33.4 %all-to-all-done.1 = bf16[32,176,128]{2,1,0:T(8,128)(2,1)S(1)} async-done(((bf16[32,176,128]{2,1,0:T(8,128)(2,1)}), bf16[32,176,128]{2,1,0:T(8,128)(2,1)S(1)}, u32[]{:S(2)}, u32[]{:S(2)}) %all-to-all-start.1) | async-done | bytes 1441824 | tf_op jit(solution)/shard_map/all_to_all | solution.py:337
  105.8 43.7 %conditional.1 = (bf16[104,32,704]{2,1,0:T(8,128)(2,1)}) conditional(s32[]{:T(128)} %convert_element_type.15, (s32[104]{0:T(128)S(1)}, s32[256]{0:T(256)S(1)}, s32[8]{0:T(128)S(1)}, s32[1]{0:T(128)}, bf16[32,176,128]{2,1,0:T(8,128)(2,1)S(1)}) %tuple.18, (s32[104]{0:T(128)S(1)}, s32[256]{0:T(256)S(1)}, s32[8]{0:T(128)S(1)}, s32[1]{0:T(128)}, ...), branch_computations={%region_5.6_spmd, %region_6.7_spmd} | conditional | bytes 43254288 | solution.py:339
  105.8 0.7 select_blocks.3.refs_0_
  106.6 1.5 collective-permute-start
  108.1 3.9 %collective-permute-start.1 = (bf16[9,176,128]{2,1,0:T(8,128)(2,1)S(1)}, bf16[9,176,128]{2,1,0:T(8,128)(2,1)S(1)}, u32[]{:S(2)}, u32[]{:S(2)}) collective-permute-start(bf16[9,176,128]{2,1,0:T(8,128)(2,1)S(1)} %slice.15), channel_id=1, source_target_pairs={{0,192},{1,193},{2,194},{3,195},{4,196},{5,197},{6,198},{7,199},{8... | collective-permute-start | bytes 1216520 | tf_op jit(solution)/shard_map/cond/branch_1_fun/ppermute | solution.py:38
  111.9 1.4 collective-permute-start.3
  113.4 0.0 collective-permute-start.2
  113.4 6.6 %collective-permute-done.refs_1_ = bf16[10,176,128]{2,1,0:T(8,128)(2,1)S(1)} collective-permute-done((bf16[10,176,128]{2,1,0:T(8,128)(2,1)S(1)}, bf16[10,176,128]{2,1,0:T(8,128)(2,1)S(1)}, u32[]{:S(2)}, u32[]{:S(2)}) %collective-permute-start) | collective-permute-done | bytes 450592 | tf_op jit(solution)/shard_map/cond/branch_1_fun/ppermute | solution.py:38
  120.0 2.7 %collective-permute-start.5 = (bf16[9,176,128]{2,1,0:T(8,128)(2,1)S(1)}, bf16[9,176,128]{2,1,0:T(8,128)(2,1)S(1)}, u32[]{:S(2)}, u32[]{:S(2)}) collective-permute-start(bf16[9,176,128]{2,1,0:T(8,128)(2,1)S(1)} %collective-permute-done.1.refs_2_), channel_id=1, source_target_pairs={{0,192},{1,193},{2,194},{3,195},{4,196},{5,197},{6,198},{7,199},{8... | collective-permute-start | bytes 1216520 | tf_op jit(solution)/shard_map/cond/branch_1_fun/ppermute | solution.py:38
  122.7 6.4 %collective-permute-start.10 = (bf16[19,176,128]{2,1,0:T(8,128)(2,1)S(1)}, bf16[19,176,128]{2,1,0:T(8,128)(2,1)S(1)}, u32[]{:S(2)}, u32[]{:S(2)}) collective-permute-start(bf16[19,176,128]{2,1,0:T(8,128)(2,1)S(1)} %select_blocks.3.refs_0_), channel_id=1, source_target_pairs={{0,32},{1,33},{2,34},{3,35},{4,36},{5,37},{6,38},{7,39},{8,40},{9,... | collective-permute-start | bytes 2568200 | tf_op jit(solution)/shard_map/cond/branch_1_fun/ppermute | solution.py:42
  129.1 5.4 %collective-permute-start.11 = (bf16[10,176,128]{2,1,0:T(8,128)(2,1)S(1)}, bf16[10,176,128]{2,1,0:T(8,128)(2,1)S(1)}, u32[]{:S(2)}, u32[]{:S(2)}) collective-permute-start(bf16[10,176,128]{2,1,0:T(8,128)(2,1)S(1)} %collective-permute-done.refs_1_), channel_id=1, source_target_pairs={{0,32},{1,33},{2,34},{3,35},{4,36},{5,37},{6,38},{7,39},{8,40},{9,... | collective-permute-start | bytes 1351688 | tf_op jit(solution)/shard_map/cond/branch_1_fun/ppermute | solution.py:42
  134.5 0.5 collective-permute-start.12
  135.0 3.1 %place_blocks.9.refs_7_ = bf16[104,32,704]{2,1,0:T(8,128)(2,1)} custom-call(s32[256]{0:T(256)S(1)} %get-tuple-element.36.order, s32[8]{0:T(128)S(1)} %get-tuple-element.37.counts, s32[1]{0:T(128)} %get-tuple-element.38.where, bf16[19,176,128]{2,1,0:T(8,128)(2,1)S(1)} %select_blocks.3.refs_0_, bf16[10,176,128]{2,1,0:T(8,128)(2,1)S(1)} %collective-permute-done.refs_1_, ...), custom_call_target="tpu_custom_call" | custom-call | tf_op jit(solution)/shard_map/cond/branch_1_fun/place_blocks/pallas_call | solution.py:279
  138.2 0.1 collective-permute-done.4.refs_5_
  138.3 3.1 %collective-permute-start.7 = (bf16[10,176,128]{2,1,0:T(8,128)(2,1)S(1)}, bf16[10,176,128]{2,1,0:T(8,128)(2,1)S(1)}, u32[]{:S(2)}, u32[]{:S(2)}) collective-permute-start(bf16[10,176,128]{2,1,0:T(8,128)(2,1)S(1)} %collective-permute-done.3.refs_4_), channel_id=1, source_target_pairs={{0,32},{1,33},{2,34},{3,35},{4,36},{5,37},{6,38},{7,39},{8,40},{9,... | collective-permute-start | bytes 1351688 | tf_op jit(solution)/shard_map/cond/branch_1_fun/ppermute | solution.py:42
  141.5 0.5 collective-permute-start.6
  142.0 0.1 collective-permute-start.9
  142.1 4.3 %place_blocks.10.refs_4_ = bf16[104,32,704]{2,1,0:T(8,128)(2,1)} custom-call(s32[256]{0:T(256)S(1)} %get-tuple-element.36.order, s32[8]{0:T(128)S(1)} %get-tuple-element.37.counts, s32[1]{0:T(128)} %get-tuple-element.38.where, bf16[19,176,128]{2,1,0:T(8,128)(2,1)S(1)} %collective-permute-done.10.refs_0_, ...), custom_call_target="tpu_custom_call", output_to_operand_aliasing={{}: (10, {})} | custom-call | tf_op jit(solution)/shard_map/cond/branch_1_fun/place_blocks/pallas_call | solution.py:279
  146.4 3.1 %place_blocks.11 = bf16[104,32,704]{2,1,0:T(8,128)(2,1)} custom-call(s32[256]{0:T(256)S(1)} %get-tuple-element.36.order, s32[8]{0:T(128)S(1)} %get-tuple-element.37.counts, s32[1]{0:T(128)} %get-tuple-element.38.where, bf16[9,176,128]{2,1,0:T(8,128)(2,1)S(1)} %collective-permute-done.6.refs_0_, ...), custom_call_target="tpu_custom_call", output_to_operand_aliasing={{}: (7, {})} | custom-call | tf_op jit(solution)/shard_map/cond/branch_1_fun/place_blocks/pallas_call | solution.py:279
  (20 shorter events, 0.1 us)
Async XLA Ops:
  4.4 12.0 %copy-start.2 = (s32[104]{0:T(128)S(1)}, s32[104]{0:T(128)}, u32[]{:S(2)}) copy-start(s32[104]{0:T(128)} %owners.1) | copy-start | bytes 1252
  4.4 47.5 %copy-start = (bf16[1,1024,704]{1,2,0:T(8,128)(2,1)S(1)}, bf16[1,1024,704]{1,2,0:T(8,128)(2,1)}, u32[]{:S(2)}) copy-start(bf16[1,1024,704]{1,2,0:T(8,128)(2,1)} %param.6) | copy-start | bytes 4325380
  4.4 47.5 %all-to-all-start = ((bf16[32,176,128]{2,1,0:T(8,128)(2,1)}), bf16[32,176,128]{2,1,0:T(8,128)(2,1)S(1)}, u32[]{:S(2)}, u32[]{:S(2)}) async-start(bf16[32,176,128]{2,1,0:T(8,128)(2,1)} %pack_rows.1), calls=%async_computation | async-start | bytes 2883584 | tf_op jit(solution)/shard_map/all_to_all | solution.py:323
  63.7 1.1 copy-start.1
  64.8 41.0 %all-to-all-start.1 = ((bf16[32,176,128]{2,1,0:T(8,128)(2,1)}), bf16[32,176,128]{2,1,0:T(8,128)(2,1)S(1)}, u32[]{:S(2)}, u32[]{:S(2)}) async-start(bf16[32,176,128]{2,1,0:T(8,128)(2,1)} %copy-done.1), calls=%async_computation.1 | async-start | bytes 2883584 | tf_op jit(solution)/shard_map/all_to_all | solution.py:337
  106.6 13.4 %collective-permute-start = (bf16[10,176,128]{2,1,0:T(8,128)(2,1)S(1)}, bf16[10,176,128]{2,1,0:T(8,128)(2,1)S(1)}, u32[]{:S(2)}, u32[]{:S(2)}) collective-permute-start(bf16[10,176,128]{2,1,0:T(8,128)(2,1)S(1)} %slice.14), channel_id=1, source_target_pairs={{0,64},{1,65},{2,66},{3,67},{4,68},{5,69},{6,70},{7,71},{8,72},{9,... | collective-permute-start | bytes 1351688 | tf_op jit(solution)/shard_map/cond/branch_1_fun/ppermute | solution.py:38
  108.1 11.9 %collective-permute-start.1 = (bf16[9,176,128]{2,1,0:T(8,128)(2,1)S(1)}, bf16[9,176,128]{2,1,0:T(8,128)(2,1)S(1)}, u32[]{:S(2)}, u32[]{:S(2)}) collective-permute-start(bf16[9,176,128]{2,1,0:T(8,128)(2,1)S(1)} %slice.15), channel_id=1, source_target_pairs={{0,192},{1,193},{2,194},{3,195},{4,196},{5,197},{6,198},{7,199},{8... | collective-permute-start | bytes 1216520 | tf_op jit(solution)/shard_map/cond/branch_1_fun/ppermute | solution.py:38
  111.9 22.6 %collective-permute-start.3 = (bf16[10,176,128]{2,1,0:T(8,128)(2,1)S(1)}, bf16[10,176,128]{2,1,0:T(8,128)(2,1)S(1)}, u32[]{:S(2)}, u32[]{:S(2)}) collective-permute-start(bf16[10,176,128]{2,1,0:T(8,128)(2,1)S(1)} %slice.14), channel_id=1, source_target_pairs={{0,192},{1,193},{2,194},{3,195},{4,196},{5,197},{6,198},{7,199},{8... | collective-permute-start | bytes 1351688 | tf_op jit(solution)/shard_map/cond/branch_1_fun/ppermute | solution.py:38
  113.4 15.7 %collective-permute-start.2 = (bf16[9,176,128]{2,1,0:T(8,128)(2,1)S(1)}, bf16[9,176,128]{2,1,0:T(8,128)(2,1)S(1)}, u32[]{:S(2)}, u32[]{:S(2)}) collective-permute-start(bf16[9,176,128]{2,1,0:T(8,128)(2,1)S(1)} %slice.15), channel_id=1, source_target_pairs={{0,64},{1,65},{2,66},{3,67},{4,68},{5,69},{6,70},{7,71},{8,72},{9,... | collective-permute-start | bytes 1216520 | tf_op jit(solution)/shard_map/cond/branch_1_fun/ppermute | solution.py:38
  120.0 18.3 %collective-permute-start.4 = (bf16[10,176,128]{2,1,0:T(8,128)(2,1)S(1)}, bf16[10,176,128]{2,1,0:T(8,128)(2,1)S(1)}, u32[]{:S(2)}, u32[]{:S(2)}) collective-permute-start(bf16[10,176,128]{2,1,0:T(8,128)(2,1)S(1)} %collective-permute-done.refs_1_), channel_id=1, source_target_pairs={{0,64},{1,65},{2,66},{3,67},{4,68},{5,69},{6,70},{7,71},{8,72},{9,... | collective-permute-start | bytes 1351688 | tf_op jit(solution)/shard_map/cond/branch_1_fun/ppermute | solution.py:38
  120.0 18.2 %collective-permute-start.5 = (bf16[9,176,128]{2,1,0:T(8,128)(2,1)S(1)}, bf16[9,176,128]{2,1,0:T(8,128)(2,1)S(1)}, u32[]{:S(2)}, u32[]{:S(2)}) collective-permute-start(bf16[9,176,128]{2,1,0:T(8,128)(2,1)S(1)} %collective-permute-done.1.refs_2_), channel_id=1, source_target_pairs={{0,192},{1,193},{2,194},{3,195},{4,196},{5,197},{6,198},{7,199},{8... | collective-permute-start | bytes 1216520 | tf_op jit(solution)/shard_map/cond/branch_1_fun/ppermute | solution.py:38
  122.7 19.4 %collective-permute-start.10 = (bf16[19,176,128]{2,1,0:T(8,128)(2,1)S(1)}, bf16[19,176,128]{2,1,0:T(8,128)(2,1)S(1)}, u32[]{:S(2)}, u32[]{:S(2)}) collective-permute-start(bf16[19,176,128]{2,1,0:T(8,128)(2,1)S(1)} %select_blocks.3.refs_0_), channel_id=1, source_target_pairs={{0,32},{1,33},{2,34},{3,35},{4,36},{5,37},{6,38},{7,39},{8,40},{9,... | collective-permute-start | bytes 2568200 | tf_op jit(solution)/shard_map/cond/branch_1_fun/ppermute | solution.py:42
  129.1 12.9 %collective-permute-start.11 = (bf16[10,176,128]{2,1,0:T(8,128)(2,1)S(1)}, bf16[10,176,128]{2,1,0:T(8,128)(2,1)S(1)}, u32[]{:S(2)}, u32[]{:S(2)}) collective-permute-start(bf16[10,176,128]{2,1,0:T(8,128)(2,1)S(1)} %collective-permute-done.refs_1_), channel_id=1, source_target_pairs={{0,32},{1,33},{2,34},{3,35},{4,36},{5,37},{6,38},{7,39},{8,40},{9,... | collective-permute-start | bytes 1351688 | tf_op jit(solution)/shard_map/cond/branch_1_fun/ppermute | solution.py:42
  134.5 6.9 %collective-permute-start.12 = (bf16[9,176,128]{2,1,0:T(8,128)(2,1)S(1)}, bf16[9,176,128]{2,1,0:T(8,128)(2,1)S(1)}, u32[]{:S(2)}, u32[]{:S(2)}) collective-permute-start(bf16[9,176,128]{2,1,0:T(8,128)(2,1)S(1)} %collective-permute-done.1.refs_2_), channel_id=1, source_target_pairs={{0,32},{1,33},{2,34},{3,35},{4,36},{5,37},{6,38},{7,39},{8,40},{9,... | collective-permute-start | bytes 1216520 | tf_op jit(solution)/shard_map/cond/branch_1_fun/ppermute | solution.py:42
  138.3 8.0 %collective-permute-start.7 = (bf16[10,176,128]{2,1,0:T(8,128)(2,1)S(1)}, bf16[10,176,128]{2,1,0:T(8,128)(2,1)S(1)}, u32[]{:S(2)}, u32[]{:S(2)}) collective-permute-start(bf16[10,176,128]{2,1,0:T(8,128)(2,1)S(1)} %collective-permute-done.3.refs_4_), channel_id=1, source_target_pairs={{0,32},{1,33},{2,34},{3,35},{4,36},{5,37},{6,38},{7,39},{8,40},{9,... | collective-permute-start | bytes 1351688 | tf_op jit(solution)/shard_map/cond/branch_1_fun/ppermute | solution.py:42
  141.4 4.9 %collective-permute-start.8 = (bf16[10,176,128]{2,1,0:T(8,128)(2,1)S(1)}, bf16[10,176,128]{2,1,0:T(8,128)(2,1)S(1)}, u32[]{:S(2)}, u32[]{:S(2)}) collective-permute-start(bf16[10,176,128]{2,1,0:T(8,128)(2,1)S(1)} %collective-permute-done.4.refs_5_), channel_id=1, source_target_pairs={{0,32},{1,33},{2,34},{3,35},{4,36},{5,37},{6,38},{7,39},{8,40},{9,... | collective-permute-start | bytes 1351688 | tf_op jit(solution)/shard_map/cond/branch_1_fun/ppermute | solution.py:42
  141.5 4.9 %collective-permute-start.6 = (bf16[9,176,128]{2,1,0:T(8,128)(2,1)S(1)}, bf16[9,176,128]{2,1,0:T(8,128)(2,1)S(1)}, u32[]{:S(2)}, u32[]{:S(2)}) collective-permute-start(bf16[9,176,128]{2,1,0:T(8,128)(2,1)S(1)} %collective-permute-done.2.refs_3_), channel_id=1, source_target_pairs={{0,32},{1,33},{2,34},{3,35},{4,36},{5,37},{6,38},{7,39},{8,40},{9,... | collective-permute-start | bytes 1216520 | tf_op jit(solution)/shard_map/cond/branch_1_fun/ppermute | solution.py:42
  142.0 4.4 %collective-permute-start.9 = (bf16[9,176,128]{2,1,0:T(8,128)(2,1)S(1)}, bf16[9,176,128]{2,1,0:T(8,128)(2,1)S(1)}, u32[]{:S(2)}, u32[]{:S(2)}) collective-permute-start(bf16[9,176,128]{2,1,0:T(8,128)(2,1)S(1)} %collective-permute-done.5.refs_6_), channel_id=1, source_target_pairs={{0,32},{1,33},{2,34},{3,35},{4,36},{5,37},{6,38},{7,39},{8,40},{9,... | collective-permute-start | bytes 1216520 | tf_op jit(solution)/shard_map/cond/branch_1_fun/ppermute | solution.py:42
